TPU v7x, 32 devices: a whole 2x2x4 slice. The times are simulated.
32 devices in a mesh: layer: 16 (over z, y, x), dp: 2 (over core).
Axes of the slice: x: 2, y: 2, z: 4, core: 2. Of those that a mesh axis runs over, the one named last changes fastest.
Arguments:
- states: float32 [16, 2, 24, 1536], P('layer', 'dp'), may hold values from -6 to 6
- adjoints: float32 [16, 2, 24, 1536], P('layer', 'dp'), may hold values from -6 to 6
- kernels: bfloat16 [64, 3, 3, 64, 64], P('layer'), may hold values from -0.25 to 0.25
- biases: float32 [64, 64], P('layer'), may hold values from -4 to 4
- coarse_gain: float32 [16, 64], P('layer'), may hold values from 0.01 to 1
Outputs:
- states_new: float32 [16, 2, 24, 1536], P('layer', 'dp')
- adjoints_new: float32 [16, 2, 24, 1536], P('layer', 'dp')
- kernel_grad: float32 [64, 3, 3, 64, 64], P('layer')
- bias_grad: float32 [64, 64], P('layer')
All inputs are finite; a program needn't handle non-finite values.
Results may differ from a plain program's by a relative error of at most 0.0054.
Values sent between devices are 32-bit elements; how exact they have to be, the bound alone decides.
A program may use at most 64 MiB of HBM per device.

v0:
```python
import jax
import jax.numpy as jnp
from jax import lax
from jax.sharding import PartitionSpec as P

step_size = 0.5


def prefix(array, axis, combine, identity, reverse):
    length, position = (lax.axis_size(axis), lax.axis_index(axis))
    everything = jax.tree.map(lambda part: lax.all_gather(part, axis), array)
    start = jax.tree.map(
        lambda part, zero: jnp.broadcast_to(jnp.asarray(zero, part.dtype), part.shape),
        array,
        identity,
    )

    def turn(k, before):
        at = length - 1 - k if reverse else k
        reached = at > position if reverse else at < position
        new = combine(before, jax.tree.map(lambda part: part[at], everything))
        return jax.tree.map(lambda a, b: jnp.where(reached, a, b), new, before)

    return lax.fori_loop(0, length, turn, start)


def correlate(field, kernel):
    return lax.conv_general_dilated(
        field,
        kernel,
        (1, 1),
        "SAME",
        dimension_numbers=("NHWC", "HWIO", "NHWC"),
        preferred_element_type=jnp.float32,
    )


def kernel_terms(field, sens_round):
    rows_img = field.shape[1]
    cols_img = field.shape[2]
    channels = field.shape[3]
    padded = jnp.pad(field.astype(jnp.bfloat16), ((0, 0), (1, 1), (1, 1), (0, 0)))
    flat_sens = sens_round.reshape(-1, channels)
    terms = []
    for row in range(3):
        for col in range(3):
            piece = padded[:, row : row + rows_img, col : col + cols_img].reshape(-1, channels)
            terms.append(
                lax.dot_general(
                    piece, flat_sens, (((0,), (0,)), ((), ())), preferred_element_type=jnp.float32
                )
            )
    return jnp.stack(terms).reshape(3, 3, channels, channels)


def compose(earlier, later):
    return (earlier[0] * later[0], later[0] * earlier[1] + later[1])


def body(states, adjoints, kernels, biases, coarse_gain):
    count_img, rows_img, flat = (states.shape[1], states.shape[2], states.shape[3])
    channels = kernels.shape[-1]
    cols_img = flat // channels
    shape_four = (count_img, rows_img, cols_img, channels)
    position = lax.axis_index("layer")
    block_count = lax.axis_size("layer")
    images = count_img * lax.axis_size("dp")
    depth_count = kernels.shape[0]
    field = states[0].reshape(shape_four)
    path = []
    acts = []
    for depth in range(depth_count):
        activ = jnp.tanh(correlate(field.astype(jnp.bfloat16), kernels[depth]) + biases[depth])
        path.append(field)
        acts.append(activ)
        field = field + step_size * activ
    gain_row = jnp.tile(coarse_gain[0], cols_img).reshape(1, 1, flat)
    zero_row = jnp.zeros_like(gain_row)
    lead_gain = jnp.where(position == 0, zero_row, gain_row)
    offset = field.reshape(count_img, rows_img, flat) - lead_gain * states[0]
    identity = (jnp.ones_like(gain_row), jnp.zeros_like(offset))
    prefix_gain, prefix_sum = prefix((lead_gain, offset), "layer", compose, identity, False)
    states_new = (prefix_gain * states[0] + prefix_sum)[None]
    adjoint = adjoints[0].reshape(shape_four)
    kgrads = [None] * depth_count
    bgrads = [None] * depth_count
    for depth in reversed(range(depth_count)):
        sens = step_size * (1.0 - acts[depth] * acts[depth]) * adjoint
        sens_round = sens.astype(jnp.bfloat16)
        flipped = kernels[depth][::-1, ::-1].transpose(0, 1, 3, 2)
        adjoint = adjoint + correlate(sens_round, flipped)
        kernel_term = kernel_terms(path[depth], sens_round)
        bias_term = jnp.sum(sens, axis=(0, 1, 2))
        kgrads[depth] = kernel_term
        bgrads[depth] = bias_term
    kernel_grad = jnp.stack(kgrads)
    bias_grad = jnp.stack(bgrads)
    kernel_grad, bias_grad = lax.psum((kernel_grad, bias_grad), "dp")
    tail_gain = jnp.where(position == block_count - 1, zero_row, gain_row)
    tail_offset = adjoint.reshape(count_img, rows_img, flat) - tail_gain * adjoints[0]
    suffix_gain, suffix_sum = prefix((tail_gain, tail_offset), "layer", compose, identity, True)
    adjoints_new = (tail_gain * suffix_sum + tail_offset)[None]
    return (states_new, adjoints_new, kernel_grad / images, bias_grad / images)


def solution(mesh):
    return jax.shard_map(
        body,
        mesh=mesh,
        in_specs=(
            P("layer", "dp", None, None),
            P("layer", "dp", None, None),
            P("layer", None, None, None, None),
            P("layer", None),
            P("layer", None),
        ),
        out_specs=(
            P("layer", "dp", None, None),
            P("layer", "dp", None, None),
            P("layer", None, None, None, None),
            P("layer", None),
        ),
        check_vma=False,
    )
```

profile of v0, /device:TPU:0, one launch (start us, length us, event | category | flops | bytes accessed | tf_op | source)
XLA Modules:
  0.0 193.8 jit_solution(4802946766550394200)
XLA Ops:
  8.1 1.1 reshape_squeeze.6
  10.5 1.2 subtract_multiply_fusion.2
  14.1 1.2 subtract_multiply_fusion
  33.4 1.2 pad_maximum_fusion
  35.4 1.5 convolution_select_fusion
  38.5 2.6 %psum.15 = f32[4,64]{1,0:T(4,128)S(1)} all-reduce(f32[4,64]{1,0:T(4,128)S(1)} %pad_maximum_fusion.1), channel_id=1, replica_groups=mesh['layer'=16,'dp'=2] {'dp'}, use_global_device_ids=true, to_apply=%region_9.10 | all-reduce | flops 256 | bytes 2048 | tf_op jit(solution)/shard_map/psum | solution.py:98
  41.7 43.0 %all_gather.16 = f32[16,1,1,1536]{3,2,1,0:T(1,128)S(1)} all-gather(f32[1,1,1,1536]{3,2,1,0:T(1,128)S(1)} %select_n.132), channel_id=1, replica_groups=mesh['layer'=16,'dp'=2] {'layer'}, dimensions={0}, use_global_device_ids=true | all-gather | bytes 104448 | tf_op jit(solution)/shard_map/all_gather | solution.py:11
  84.6 36.1 %all_gather.18 = f32[16,1,1,1536]{3,2,1,0:T(1,128)S(1)} all-gather(f32[1,1,1,1536]{3,2,1,0:T(1,128)S(1)} %select_n.138), channel_id=1, replica_groups=mesh['layer'=16,'dp'=2] {'layer'}, dimensions={0}, use_global_device_ids=true | all-gather | bytes 104448 | tf_op jit(solution)/shard_map/all_gather | solution.py:11
  120.7 2.4 %broadcast_multiply_fusion = f32[4,3,3,64,64]{4,3,2,1,0:T(8,128)} fusion(f32[4,3,3,64,64]{4,3,2,1,0:T(8,128)} %all-reduce.6.cloned.1.call-done), kind=kLoop, calls=%fused_computation.106 | loop fusion | flops 147456 | bytes 1179648 | tf_op jit(solution)/shard_map/div | solution.py:103
  123.2 17.1 %while.32 = (s32[]{:T(128)}, f32[1,1,1536]{2,1,0:T(1,128)S(1)}, f32[1,24,1536]{2,1,0:T(8,128)S(1)}, s32[]{:T(128)}, f32[16,1,1,1536]{3,2,1,0:T(1,128)S(1)}, /*in...) while((s32[]{:T(128)}, f32[1,1,1536]{2,1,0:T(1,128)S(1)}, f32[1,24,1536]{2,1,0:T(8,128)S(1)}, ...), condition=%wide.region_1.2_spmd.clone, body=%wide.region_0.1_spmd.clone.sunk | while | flops 152068 | bytes 479351 | solution.py:24
  123.2 1.0 fusion.321
  126.4 1.0 fusion.321
  130.7 1.0 fusion.321
  139.3 1.0 fusion.321
  140.3 28.4 %all-gather.5.cloned.1.call-done = f32[16,1,24,1536]{3,2,1,0:T(8,128)} async-done(((f32[1,1,24,1536]{3,2,1,0:T(8,128)}), f32[16,1,24,1536]{3,2,1,0:T(8,128)}) %all-gather.5.cloned.1.call-update) | async-done | bytes 2359312 | tf_op jit(solution)/shard_map/all_gather | solution.py:11
  168.7 16.9 %while.33 = (s32[]{:T(128)}, f32[1,24,1536]{2,1,0:T(8,128)S(1)}, s32[]{:T(128)}, f32[16,1,1,1536]{3,2,1,0:T(1,128)S(1)}, f32[16,1,24,1536]{3,2,1,0:T(8,128)}, /*index=5*/s32[]{:T(128)}, s32[]{:T(128)}, s32[]{:T(128)}, s32[]{:T(128)}) while((s32[]{:T(128)}, f32[1,24,1536]{2,1,0:T(8,128)S(1)}, s32[]{:T(128)}, ...), condition=%wide.region_3.4_spmd.clone, body=%wide.region_2.3_spmd.clone.sunk | while | flops 147464 | bytes 460967 | solution.py:24
  168.8 1.0 fusion.322
  169.8 1.0 fusion.322
  170.9 1.0 fusion.322
  171.9 1.0 fusion.322
  173.0 1.0 fusion.322
  174.0 1.0 fusion.322
  175.1 1.0 fusion.322
  176.2 1.0 fusion.322
  177.2 1.0 fusion.322
  178.3 1.0 fusion.322
  179.3 1.0 fusion.322
  180.4 1.0 fusion.322
  181.4 1.0 fusion.322
  182.5 1.0 fusion.322
  183.6 1.0 fusion.322
  184.6 1.0 fusion.322
  (226 shorter events, 37.7 us)
Async XLA Ops:
  8.0 1.4 copy-start.13
  8.0 1.4 copy-start.8
  8.0 1.4 copy-start.10
  8.0 112.7 %all-reduce.6.cloned.1.call-start = ((), (), s32[]{:S(2)}) async-start(), calls=%async_computation.2 | async-start | bytes 2359296 | tf_op jit(solution)/shard_map/psum | solution.py:98
  12.0 1.1 copy-start.11
  15.3 0.9 copy-start
  16.3 1.1 copy-start.12
  19.7 1.0 copy-start.3
  23.5 1.0 copy-start.2
  24.5 0.7 copy-start.6
  24.8 0.7 copy-start.9
  24.8 0.9 copy-start.1
  25.3 1.2 copy-start.7
  26.4 1.3 copy-start.5
  28.2 1.4 copy-start.4
  34.6 88.6 %all-gather.3.cloned.1.call-start = ((), (), s32[]{:S(2)}) async-start(), calls=%async_computation | async-start | bytes 2506752 | tf_op jit(solution)/shard_map/all_gather | solution.py:11
  35.1 133.6 %all-gather.5.cloned.1.call-start = ((), (), s32[]{:S(2)}) async-start(), calls=%async_computation.1 | async-start | bytes 2506752 | tf_op jit(solution)/shard_map/all_gather | solution.py:11
Sparse Core Ops, SparseCore 0:
  34.7 22.4 all-reduce.5
Sparse Core Ops, SparseCore 1:
  38.4 65.6 all-gather.2
  107.3 61.4 all-gather.4
where the time goes:
time: 195 us; the launch traced here: 194 us
  blocking collectives  81.6 us (42%)
  other arithmetic  39.4 us (20%)
  waiting for transfers between devices  29 us (15%)
  between operations  16.4 us (8%)
  matrix products  16.1 us (8%)
  local copies, waits for them, and re-layouts  9.91 us (5%)
    all_gather x2, blocking collectives, prefix(): everything = jax.tree.map(lambda part: lax.all_gather(part, axis), array)  79.1 us
    select_n x48, other arithmetic, turn(): return jax.tree.map(lambda a, b: jnp.where(reached, a, b), new, before)  32 us
    all_gather x2, waiting for transfers between devices, prefix(): everything = jax.tree.map(lambda part: lax.all_gather(part, axis), array)  28.4 us
    dot_general x36, matrix products, kernel_terms(): lax.dot_general(piece, flat_sens, (((0,), (0,)), ((), ())), preferred_ele...  9.38 us
    conv_general_dilated x8, matrix products, correlate(): lax.conv_general_dilated(field, kernel, (1, 1), 'SAME', dimension_numbers...  6.76 us
  transfers between devices with their start and end apart: 3, of which 1 were waited for; matrix products, arithmetic and copies ran while one was open for 12% of the time, Pallas kernels for 0%

commit v1 on v0

v1 whole, which is shorter than its diff:
```python
import functools

import jax
import jax.numpy as jnp
from jax import lax
from jax.experimental import pallas as pl
from jax.experimental.pallas import tpu as pltpu
from jax.sharding import PartitionSpec as P

step_size = 0.5
MESH = pl.DeviceIdType.MESH
F32 = jnp.float32
BF16 = jnp.bfloat16


def down(array, count):
    zero = jnp.zeros((count, array.shape[1]), array.dtype)
    return jnp.concatenate([zero, array[:-count]], axis=0)


def up(array, count):
    zero = jnp.zeros((count, array.shape[1]), array.dtype)
    return jnp.concatenate([array[count:], zero], axis=0)


def pack(array):
    half = array.shape[0] // 2
    return jnp.concatenate([array[:half], array[half:]], axis=1)


def kernel(
    n, m, c, owners, cols, images,
    st, adj, ker, bias, gain,
    out_s, out_a, out_k, out_b,
    xs, acts, s3s, kf, fsend, asend, fin, ain, fout, aout, fres, ares, gbuf,
    fs_send, fs_recv, as_send, as_recv, fr_send, fr_recv, ar_send, ar_recv, g_send, g_recv,
):
    me = lax.axis_index("layer")
    mine = lax.axis_index("dp")
    depth_count = ker.shape[0]
    ch = ker.shape[-1]
    cells = st.shape[0]
    half = cells // 2

    barrier = pltpu.get_barrier_semaphore()

    def greet(k, carry):
        pl.semaphore_signal(
            barrier, inc=1, device_id={"layer": lax.rem(me + k, n)}, device_id_type=MESH
        )
        return carry

    def greet_dp(k, carry):
        pl.semaphore_signal(
            barrier, inc=1, device_id={"dp": lax.rem(mine + k, m)}, device_id_type=MESH
        )
        return carry

    lax.fori_loop(1, n, greet, 0)
    lax.fori_loop(1, m, greet_dp, 0)

    column = lax.rem(lax.broadcasted_iota(jnp.int32, (cells, ch), 0), cols)
    has_left = column > 0
    has_right = column < cols - 1

    for d in range(depth_count):
        kf[d] = jnp.concatenate(
            [
                jnp.concatenate([ker[d, dy, dx] for dx in range(3)], axis=0)
                for dy in range(3)
            ],
            axis=1,
        )

    field = st[...]
    for d in range(depth_count):
        left = jnp.where(has_left, down(field, 1), 0.0)
        right = jnp.where(has_right, up(field, 1), 0.0)
        x = jnp.concatenate([left, field, right], axis=1).astype(BF16)
        xs[d] = x
        y = jnp.dot(x, kf[d], preferred_element_type=F32)
        total = down(y[:, :ch], cols) + y[:, ch : 2 * ch] + up(y[:, 2 * ch :], cols)
        act = jnp.tanh(total + bias[d : d + 1, :])
        acts[d] = act
        field = field + step_size * act

    gain_row = gain[...]
    zero_row = jnp.zeros_like(gain_row)
    lead = jnp.where(me == 0, zero_row, gain_row)
    tail = jnp.where(me == n - 1, zero_row, gain_row)
    gain_two = jnp.concatenate([gain_row, gain_row], axis=1)

    pl.semaphore_wait(barrier, n - 1 + m - 1)

    def scatter(src, dst, send, recv, peer):
        return pltpu.make_async_remote_copy(
            src_ref=src.at[peer], dst_ref=dst.at[me],
            send_sem=send.at[peer], recv_sem=recv.at[me],
            device_id={"layer": peer}, device_id_type=MESH,
        )

    def arrived(dst, send, recv, source):
        pltpu.make_async_remote_copy(
            src_ref=dst.at[source], dst_ref=dst.at[source],
            send_sem=send.at[source], recv_sem=recv.at[source],
            device_id={"layer": source}, device_id_type=MESH,
        ).wait_recv()

    def scatter_all(src, dst, send, recv):
        def go(k, carry):
            peer = lax.rem(me + k, n)

            @pl.when(peer < owners)
            def _():
                scatter(src, dst, send, recv, peer).start()

            return carry

        lax.fori_loop(1, n, go, 0)

    def scatter_sent(src, dst, send, recv):
        def go(k, carry):
            peer = lax.rem(me + k, n)

            @pl.when(peer < owners)
            def _():
                scatter(src, dst, send, recv, peer).wait_send()

            return carry

        lax.fori_loop(1, n, go, 0)

    def arrived_all(dst, send, recv):
        def go(k, carry):
            arrived(dst, send, recv, lax.rem(me + k, n))
            return carry

        lax.fori_loop(1, n, go, 0)

    def give_all(src, dst, send, recv):
        def go(k, carry):
            scatter(src, dst, send, recv, lax.rem(me + k, n)).start()
            return carry

        lax.fori_loop(1, n, go, 0)

    def given_all(src, dst, send, recv):
        def go(k, carry):
            scatter(src, dst, send, recv, lax.rem(me + k, n)).wait_send()
            return carry

        lax.fori_loop(1, n, go, 0)

    def taken_all(dst, send, recv):
        def go(k, carry):
            source = lax.rem(me + k, n)

            @pl.when(source < owners)
            def _():
                arrived(dst, send, recv, source)

            return carry

        lax.fori_loop(1, n, go, 0)

    fsend[:, :c] = pack(field - lead * st[...]).reshape(owners, c, 2 * ch)
    fsend[:, c:] = jnp.broadcast_to(gain_two[None], (owners, 8, 2 * ch))
    scatter_all(fsend, fin, fs_send, fs_recv)

    lam = adj[...]
    for d in reversed(range(depth_count)):
        act = acts[d]
        sens = step_size * (1.0 - act * act) * lam
        total = jnp.sum(sens, axis=0, keepdims=True)
        gbuf[mine, d, 3 * ch :, :] = jnp.broadcast_to(
            jnp.concatenate([total, total, total], axis=1), (8, 3 * ch)
        )
        s3 = jnp.concatenate([up(sens, cols), sens, down(sens, cols)], axis=1).astype(BF16)
        s3s[d] = s3
        t = lax.dot_general(s3, kf[d], (((1,), (1,)), ((), ())), preferred_element_type=F32)
        lam = (
            lam
            + t[:, ch : 2 * ch]
            + jnp.where(has_right, up(t[:, :ch], 1), 0.0)
            + jnp.where(has_left, down(t[:, 2 * ch :], 1), 0.0)
        )

    asend[...] = pack(lam - tail * adj[...]).reshape(owners, c, 2 * ch)
    scatter_all(asend, ain, as_send, as_recv)

    @pl.when(me < owners)
    def _():
        fin[me] = fsend[me]
        ain[me] = asend[me]
        arrived_all(fin, fs_send, fs_recv)

        def turn(k, run):
            fout[k] = run
            part = fin[k]
            return part[c : c + 1] * run + part[:c]

        lax.fori_loop(0, n, turn, jnp.zeros((c, 2 * ch), F32))
        fres[me] = fout[me]
        give_all(fout, fres, fr_send, fr_recv)

    def pair(d, peer):
        return pltpu.make_async_remote_copy(
            src_ref=gbuf.at[mine, d], dst_ref=gbuf.at[mine, d],
            send_sem=g_send.at[peer, d], recv_sem=g_recv.at[mine, d],
            device_id={"dp": peer}, device_id_type=MESH,
        )

    def share(d):
        gbuf[mine, d, : 3 * ch, :] = lax.dot_general(
            xs[d], s3s[d], (((0,), (0,)), ((), ())), preferred_element_type=F32
        )

        def go(k, carry):
            pair(d, lax.rem(mine + k, m)).start()
            return carry

        lax.fori_loop(1, m, go, 0)

    for d in range(depth_count // 2):
        share(d)

    @pl.when(me < owners)
    def _():
        arrived_all(ain, as_send, as_recv)

        def turn(k, run):
            at = n - 1 - k
            new = fin[at, c : c + 1, :] * run + ain[at]
            aout[at] = new
            return new

        lax.fori_loop(0, n, turn, jnp.zeros((c, 2 * ch), F32))
        ares[me] = aout[me]
        give_all(aout, ares, ar_send, ar_recv)

    for d in range(depth_count // 2, depth_count):
        share(d)

    taken_all(fres, fr_send, fr_recv)
    new = fres[...].reshape(half, 2 * ch)

    @pl.when(me == 0)
    def _():
        out_s[...] = st[...]

    @pl.when(me > 0)
    def _():
        out_s[:half] = new[:, :ch]
        out_s[half:] = new[:, ch:]

    for d in range(depth_count):

        def go(k, carry):
            source = lax.rem(mine + k, m)
            pltpu.make_async_remote_copy(
                src_ref=gbuf.at[source, d], dst_ref=gbuf.at[source, d],
                send_sem=g_send.at[source, d], recv_sem=g_recv.at[source, d],
                device_id={"dp": source}, device_id_type=MESH,
            ).wait_recv()
            return carry

        lax.fori_loop(1, m, go, 0)
        total = gbuf[0, d]
        for k in range(1, m):
            total = total + gbuf[k, d]
        total = total * (1.0 / images)
        for dy in range(3):
            for dx in range(3):
                out_k[d, dy, dx] = total[dx * ch : (dx + 1) * ch, dy * ch : (dy + 1) * ch]
        out_b[d : d + 1, :] = total[3 * ch : 3 * ch + 1, :ch]

    taken_all(ares, ar_send, ar_recv)
    new = ares[...].reshape(half, 2 * ch)
    out_a[:half] = new[:, :ch]
    out_a[half:] = new[:, ch:]

    scatter_sent(fsend, fin, fs_send, fs_recv)
    scatter_sent(asend, ain, as_send, as_recv)

    @pl.when(me < owners)
    def _():
        given_all(fout, fres, fr_send, fr_recv)
        given_all(aout, ares, ar_send, ar_recv)

    for d in range(depth_count):

        def gone(k, carry):
            pair(d, lax.rem(mine + k, m)).wait_send()
            return carry

        lax.fori_loop(1, m, gone, 0)


def body(states, adjoints, kernels, biases, coarse_gain):
    rows, flat = states.shape[2], states.shape[3]
    depth_count, ch = kernels.shape[0], kernels.shape[-1]
    cols = flat // ch
    cells = rows * cols
    half = cells // 2
    n, m = lax.axis_size("layer"), lax.axis_size("dp")
    images = m * states.shape[1]
    c = next(k for k in range(8, half + 1, 8) if half % k == 0 and half // k <= n)
    owners = half // c
    vmem = pl.BlockSpec(memory_space=pltpu.VMEM)
    wide = 2 * ch
    dma = pltpu.SemaphoreType.DMA
    new_s, new_a, kgrad, bgrad = pl.pallas_call(
        functools.partial(kernel, n, m, c, owners, cols, images),
        out_shape=(
            jax.ShapeDtypeStruct((cells, ch), F32),
            jax.ShapeDtypeStruct((cells, ch), F32),
            jax.ShapeDtypeStruct(kernels.shape, F32),
            jax.ShapeDtypeStruct(biases.shape, F32),
        ),
        in_specs=[vmem] * 5,
        out_specs=(vmem,) * 4,
        scratch_shapes=[
            pltpu.VMEM((depth_count, cells, 3 * ch), BF16),
            pltpu.VMEM((depth_count, cells, ch), F32),
            pltpu.VMEM((depth_count, cells, 3 * ch), BF16),
            pltpu.VMEM((depth_count, 3 * ch, 3 * ch), BF16),
            pltpu.VMEM((owners, c + 8, wide), F32),
            pltpu.VMEM((owners, c, wide), F32),
            pltpu.VMEM((n, c + 8, wide), F32),
            pltpu.VMEM((n, c, wide), F32),
            pltpu.VMEM((n, c, wide), F32),
            pltpu.VMEM((n, c, wide), F32),
            pltpu.VMEM((owners, c, wide), F32),
            pltpu.VMEM((owners, c, wide), F32),
            pltpu.VMEM((m, depth_count, 3 * ch + 8, 3 * ch), F32),
        ]
        + [dma((n,))] * 8
        + [dma((m, depth_count))] * 2,
        compiler_params=pltpu.CompilerParams(
            collective_id=0, has_side_effects=True, vmem_limit_bytes=48 * 1024 * 1024
        ),
    )(
        states.reshape(cells, ch),
        adjoints.reshape(cells, ch),
        kernels,
        biases,
        coarse_gain,
    )
    return (
        new_s.reshape(states.shape),
        new_a.reshape(states.shape),
        kgrad,
        bgrad,
    )


def solution(mesh):
    return jax.shard_map(
        body,
        mesh=mesh,
        in_specs=(
            P("layer", "dp", None, None),
            P("layer", "dp", None, None),
            P("layer", None, None, None, None),
            P("layer", None),
            P("layer", None),
        ),
        out_specs=(
            P("layer", "dp", None, None),
            P("layer", "dp", None, None),
            P("layer", None, None, None, None),
            P("layer", None),
        ),
        check_vma=False,
    )
```

time: 195 us -> 32.8 us (0.17)
  the two profiles are of different devices: /device:TPU:0 before, /device:TPU:24 now
where the time goes in v1:
time: 32.8 us; the launch traced here: 32.6 us
  Pallas kernels  25.3 us (77%)
  local copies, waits for them, and re-layouts  6.58 us (20%)
  between operations  0.67 us (2%)
    pallas_call x1, Pallas kernels, body(): pl.pallas_call(functools.partial(kernel, n, m, c, owners, cols, images),...  25.3 us
    unnamed x8, local copies, waits for them, and re-layouts  2.93 us
    reshape x1, local copies, waits for them, and re-layouts, body(): states.reshape(cells, ch)  1.08 us
    reshape x1, local copies, waits for them, and re-layouts, body(): adjoints.reshape(cells, ch)  1.02 us
    reshape x1, local copies, waits for them, and re-layouts, body(): new_s.reshape(states.shape)  0.78 us
    reshape x1, local copies, waits for them, and re-layouts, body(): new_a.reshape(states.shape)  0.78 us

profile of v1, /device:TPU:24, one launch (start us, length us, event | category | flops | bytes accessed | tf_op | source)
XLA Modules:
  0.0 32.6 jit_solution(10480753203035026429)
XLA Ops:
  0.6 0.0 copy-start
  0.6 1.1 %reshape.20.st = f32[576,64]{1,0:T(8,128)S(1)} reshape(f32[1,1,24,1536]{3,2,1,0:T(8,128)} %param.5) | data formatting | bytes 294912 | tf_op jit(solution)/shard_map/reshape | solution.py:343
  1.7 1.0 %reshape.21.adj = f32[576,64]{1,0:T(8,128)S(1)} reshape(f32[1,1,24,1536]{3,2,1,0:T(8,128)} %param.6) | data formatting | bytes 294912 | tf_op jit(solution)/shard_map/reshape | solution.py:344
  2.7 0.0 copy-done
  2.7 0.0 copy-start.1
  2.8 0.7 %copy-done.1 = f32[4,64]{1,0:T(4,128)S(1)} copy-done((f32[4,64]{1,0:T(4,128)S(1)}, f32[4,64]{1,0:T(4,128)}, u32[]{:S(2)}) %copy-start.1) | copy-done | bytes 1048
  3.4 0.0 copy-start.2
  3.4 0.7 %copy-done.2 = f32[1,64]{1,0:T(1,128)S(1)} copy-done((f32[1,64]{1,0:T(1,128)S(1)}, f32[1,64]{1,0:T(1,128)}, u32[]{:S(2)}) %copy-start.2) | copy-done | bytes 280
  4.1 25.3 %shard_map.84 = (f32[576,64]{1,0:T(8,128)S(1)}, f32[576,64]{1,0:T(8,128)S(1)}, f32[4,3,3,64,64]{4,3,2,1,0:T(8,128)S(1)}, f32[4,64]{1,0:T(4,128)S(1)}) custom-call(f32[576,64]{1,0:T(8,128)S(1)} %reshape.20.st, f32[576,64]{1,0:T(8,128)S(1)} %reshape.21.adj, bf16[4,3,3,64,64]{4,3,2,1,0:T(8,128)(2,1)S(1)} %copy-done, f32[4,64]{1,0:T(4,128)S(1)} %copy-done.1, ...), custom_call_target="tpu_custom_call" | custom-call | tf_op jit(solution)/shard_map/pallas_call | solution.py:312
  29.4 0.8 %reshape.22 = f32[1,1,24,1536]{3,2,1,0:T(8,128)} reshape(f32[576,64]{1,0:T(8,128)S(1)} %get-tuple-element.8) | data formatting | bytes 294912 | tf_op jit(solution)/shard_map/reshape | solution.py:350
  30.2 0.8 %reshape.23 = f32[1,1,24,1536]{3,2,1,0:T(8,128)} reshape(f32[576,64]{1,0:T(8,128)S(1)} %get-tuple-element.9) | data formatting | bytes 294912 | tf_op jit(solution)/shard_map/reshape | solution.py:351
  31.0 1.0 %copy.11 = f32[4,3,3,64,64]{4,3,2,1,0:T(8,128)} copy(f32[4,3,3,64,64]{4,3,2,1,0:T(8,128)S(1)} %get-tuple-element.18) | data formatting | bytes 1179648
  32.0 0.6 %copy.12 = f32[4,64]{1,0:T(4,128)} copy(f32[4,64]{1,0:T(4,128)S(1)} %get-tuple-element.19) | data formatting | bytes 2048
Async XLA Ops:
  0.6 2.1 %copy-start = (bf16[4,3,3,64,64]{4,3,2,1,0:T(8,128)(2,1)S(1)}, bf16[4,3,3,64,64]{4,3,2,1,0:T(8,128)(2,1)}, u32[]{:S(2)}) copy-start(bf16[4,3,3,64,64]{4,3,2,1,0:T(8,128)(2,1)} %ker.1) | copy-start | bytes 884740
  2.7 0.7 %copy-start.1 = (f32[4,64]{1,0:T(4,128)S(1)}, f32[4,64]{1,0:T(4,128)}, u32[]{:S(2)}) copy-start(f32[4,64]{1,0:T(4,128)} %bias.1) | copy-start | bytes 3076
  3.4 0.7 %copy-start.2 = (f32[1,64]{1,0:T(1,128)S(1)}, f32[1,64]{1,0:T(1,128)}, u32[]{:S(2)}) copy-start(f32[1,64]{1,0:T(1,128)} %gain.1) | copy-start | bytes 772

commit v2 on v1

v2 whole, which is shorter than its diff:
```python
import functools

import jax
import jax.numpy as jnp
from jax import lax
from jax.experimental import pallas as pl
from jax.experimental.pallas import tpu as pltpu
from jax.sharding import PartitionSpec as P

step_size = 0.5
group = 4
MESH = pl.DeviceIdType.MESH
F32 = jnp.float32
BF16 = jnp.bfloat16


def down(array, count):
    zero = jnp.zeros((count, array.shape[1]), array.dtype)
    return jnp.concatenate([zero, array[:-count]], axis=0)


def up(array, count):
    zero = jnp.zeros((count, array.shape[1]), array.dtype)
    return jnp.concatenate([array[count:], zero], axis=0)


def cells_of(array, rows, ch):
    count = array.shape[1] // ch
    return jnp.concatenate([array[:, k * ch : (k + 1) * ch] for k in range(count)], axis=0)


def pack(array, rows, dst):
    share = array.shape[0] // (2 * rows * group)
    for k in range(group * share):
        at = 2 * k * rows
        to = (k % share) * rows
        dst[k // share, to : to + rows] = jnp.concatenate(
            [array[at : at + rows], array[at + rows : at + 2 * rows]], axis=1
        )


def unpack(src, dst, rows):
    share = src.shape[1] // rows
    wide = src.shape[2]
    for k in range(group * share):
        at = (k % share) * rows
        dst[:, k * wide : (k + 1) * wide] = src[k // share, at : at + rows]


def store(out_s, out_a, out_k, out_b, to_s, to_a, to_k, to_b, sems):
    copies = [
        pltpu.make_async_copy(src, dst, sems.at[k])
        for k, (src, dst) in enumerate(
            [(out_k, to_k), (out_s, to_s.at[0, 0]), (out_a, to_a.at[0, 0]), (out_b, to_b)]
        )
    ]
    for copy in copies:
        copy.start()
    for copy in copies:
        copy.wait()


def kernel(
    n, m, c, images,
    st_any, adj_any, ker_any, bias_any, gain_any,
    out_s, out_a, out_k, out_b,
    st, adj, ker, bias, gain, in_sem,
    xs, acts, s3s, kf, fsend, asend, fin, ain, fcomp, acomp, fz, az, fout, aout, fres, ares, gbuf,
    fs_send, fs_recv, as_send, as_recv, fr_send, fr_recv, ar_send, ar_recv,
    fz_send, fz_recv, az_send, az_recv, g_send, g_recv,
):
    me = lax.axis_index("layer")
    mine = lax.axis_index("dp")
    depth_count = ker.shape[0]
    ch = ker.shape[-1]
    flat = st.shape[1]
    cells = c * flat // ch
    top = asend.shape[1]

    loads = [
        pltpu.make_async_copy(src, dst, in_sem.at[k])
        for k, (src, dst) in enumerate(
            [
                (ker_any, ker),
                (st_any.at[0, 0], st),
                (bias_any, bias),
                (adj_any.at[0, 0], adj),
                (gain_any, gain),
            ]
        )
    ]
    for load in loads:
        load.start()

    barrier = pltpu.get_barrier_semaphore()

    place = lax.rem(me, group)
    plane = me // group
    planes = n // group

    def signal(target):
        pl.semaphore_signal(barrier, inc=1, device_id=target, device_id_type=MESH)

    def greet(k, carry):
        signal({"layer": lax.rem(plane + k, planes) * group + place})
        return carry

    def greet_dp(k, carry):
        signal({"dp": lax.rem(mine + k, m)})
        return carry

    for k in range(1, group):
        signal({"layer": plane * group + lax.rem(place + k, group)})
    lax.fori_loop(1, planes, greet, 0)
    lax.fori_loop(1, m, greet_dp, 0)

    row = lax.rem(lax.broadcasted_iota(jnp.int32, (cells, ch), 0), c)
    has_left = row > 0
    has_right = row < c - 1
    loads[0].wait()

    for d in range(depth_count):
        kf[d] = jnp.concatenate(
            [
                jnp.concatenate([ker[d, dy, dx] for dy in range(3)], axis=0)
                for dx in range(3)
            ],
            axis=1,
        )

    loads[1].wait()
    start = cells_of(st[...], c, ch)
    field = start
    loads[2].wait()
    for d in range(depth_count):
        left = jnp.where(has_left, down(field, 1), 0.0)
        right = jnp.where(has_right, up(field, 1), 0.0)
        x = jnp.concatenate([left, field, right], axis=1).astype(BF16)
        xs[d] = x
        y = jnp.dot(x, kf[d], preferred_element_type=F32)
        total = down(y[:, :ch], c) + y[:, ch : 2 * ch] + up(y[:, 2 * ch :], c)
        act = jnp.tanh(total + bias[d : d + 1, :])
        acts[d] = act
        field = field + step_size * act

    loads[3].wait()
    loads[4].wait()
    gain_row = gain[...]
    zero_row = jnp.zeros_like(gain_row)
    lead = jnp.where(me == 0, zero_row, gain_row)
    tail = jnp.where(me == n - 1, zero_row, gain_row)
    gain_two = jnp.concatenate([gain_row, gain_row], axis=1)

    pl.semaphore_wait(barrier, group - 1 + planes - 1 + m - 1)

    def across(src, dst, send, recv, k):
        peer = lax.rem(place + k, group)
        return pltpu.make_async_remote_copy(
            src_ref=src.at[peer], dst_ref=dst.at[place],
            send_sem=send.at[peer], recv_sem=recv.at[place],
            device_id={"layer": plane * group + peer}, device_id_type=MESH,
        )

    def along(src, dst, send, recv, to):
        return pltpu.make_async_remote_copy(
            src_ref=src, dst_ref=dst.at[plane],
            send_sem=send.at[to], recv_sem=recv.at[plane],
            device_id={"layer": to * group + place}, device_id_type=MESH,
        )

    def arrived(dst, send, recv, slot, source):
        pltpu.make_async_remote_copy(
            src_ref=dst.at[slot], dst_ref=dst.at[slot],
            send_sem=send.at[slot], recv_sem=recv.at[slot],
            device_id={"layer": source}, device_id_type=MESH,
        ).wait_recv()

    def scatter_all(*refs):
        for k in range(1, group):
            across(*refs, k).start()

    def scatter_sent(*refs):
        for k in range(1, group):
            across(*refs, k).wait_send()

    def arrived_all(dst, send, recv):
        for k in range(1, group):
            slot = lax.rem(place + k, group)
            arrived(dst, send, recv, slot, plane * group + slot)

    def along_all(low, high, *refs):
        def go(to, carry):
            along(*refs, to).start()
            return carry

        lax.fori_loop(low, high, go, 0)

    def along_sent(low, high, *refs):
        def go(to, carry):
            along(*refs, to).wait_send()
            return carry

        lax.fori_loop(low, high, go, 0)

    def compose(parts, comp, order):
        run = parts[order[0], :top]
        all_gain = fin[order[0], top : top + 1]
        for k in order[1:]:
            step = fin[k, top : top + 1]
            run = step * run + parts[k, :top]
            all_gain = step * all_gain
        comp[:top] = run
        comp[top:] = jnp.broadcast_to(all_gain, (8, 2 * ch))

    pack(field - lead * start, c, fsend)
    fsend[:, top:] = jnp.broadcast_to(gain_two[None], (group, 8, 2 * ch))
    scatter_all(fsend, fin, fs_send, fs_recv)

    end = cells_of(adj[...], c, ch)
    lam = end
    for d in reversed(range(depth_count)):
        act = acts[d]
        sens = step_size * (1.0 - act * act) * lam
        total = jnp.sum(sens, axis=0, keepdims=True)
        gbuf[mine, d, 3 * ch :, :] = jnp.broadcast_to(
            jnp.concatenate([total, total, total], axis=1), (8, 3 * ch)
        )
        s3 = jnp.concatenate([up(sens, c), sens, down(sens, c)], axis=1).astype(BF16)
        s3s[d] = s3
        t = lax.dot_general(s3, kf[d], (((1,), (1,)), ((), ())), preferred_element_type=F32)
        lam = (
            lam
            + t[:, ch : 2 * ch]
            + jnp.where(has_right, up(t[:, :ch], 1), 0.0)
            + jnp.where(has_left, down(t[:, 2 * ch :], 1), 0.0)
        )

    pack(lam - tail * end, c, asend)
    scatter_all(asend, ain, as_send, as_recv)

    fin[place] = fsend[place]
    ain[place] = asend[place]
    arrived_all(fin, fs_send, fs_recv)
    compose(fin, fcomp, range(group))
    along_all(plane + 1, planes, fcomp, fz, fz_send, fz_recv)
    arrived_all(ain, as_send, as_recv)
    compose(ain, acomp, range(group - 1, -1, -1))
    along_all(0, plane, acomp, az, az_send, az_recv)

    def pair(d, peer):
        return pltpu.make_async_remote_copy(
            src_ref=gbuf.at[mine, d], dst_ref=gbuf.at[mine, d],
            send_sem=g_send.at[peer, d], recv_sem=g_recv.at[mine, d],
            device_id={"dp": peer}, device_id_type=MESH,
        )

    def share(d):
        gbuf[mine, d, : 3 * ch, :] = lax.dot_general(
            xs[d], s3s[d], (((0,), (0,)), ((), ())), preferred_element_type=F32
        )

        def go(k, carry):
            pair(d, lax.rem(mine + k, m)).start()
            return carry

        lax.fori_loop(1, m, go, 0)

    for d in range(depth_count):
        share(d)

    def earlier(k, run):
        arrived(fz, fz_send, fz_recv, k, k * group + place)
        return fz[k, top : top + 1] * run + fz[k, :top]

    run = lax.fori_loop(0, plane, earlier, jnp.zeros((top, 2 * ch), F32))
    for k in range(group):
        fout[k] = run
        if k < group - 1:
            run = fin[k, top : top + 1] * run + fin[k, :top]
    fres[place] = fout[place]
    scatter_all(fout, fres, fr_send, fr_recv)

    def later(k, run):
        at = planes - 1 - k
        arrived(az, az_send, az_recv, at, at * group + place)
        return az[at, top : top + 1] * run + az[at, :top]

    run = lax.fori_loop(0, planes - 1 - plane, later, jnp.zeros((top, 2 * ch), F32))
    for k in range(group - 1, -1, -1):
        run = fin[k, top : top + 1] * run + ain[k]
        aout[k] = run
    ares[place] = aout[place]
    scatter_all(aout, ares, ar_send, ar_recv)

    arrived_all(fres, fr_send, fr_recv)

    @pl.when(me == 0)
    def _():
        out_s[...] = st[...]

    @pl.when(me > 0)
    def _():
        unpack(fres, out_s, c)

    for d in range(depth_count):

        def go(k, carry):
            source = lax.rem(mine + k, m)
            pltpu.make_async_remote_copy(
                src_ref=gbuf.at[source, d], dst_ref=gbuf.at[source, d],
                send_sem=g_send.at[source, d], recv_sem=g_recv.at[source, d],
                device_id={"dp": source}, device_id_type=MESH,
            ).wait_recv()
            return carry

        lax.fori_loop(1, m, go, 0)
        total = gbuf[0, d]
        for k in range(1, m):
            total = total + gbuf[k, d]
        total = total * (1.0 / images)
        for dy in range(3):
            for dx in range(3):
                out_k[d, dy, dx] = total[dy * ch : (dy + 1) * ch, dx * ch : (dx + 1) * ch]
        out_b[d : d + 1, :] = total[3 * ch : 3 * ch + 1, :ch]

    arrived_all(ares, ar_send, ar_recv)
    unpack(ares, out_a, c)

    scatter_sent(fsend, fin, fs_send, fs_recv)
    scatter_sent(asend, ain, as_send, as_recv)
    scatter_sent(fout, fres, fr_send, fr_recv)
    scatter_sent(aout, ares, ar_send, ar_recv)
    along_sent(plane + 1, planes, fcomp, fz, fz_send, fz_recv)
    along_sent(0, plane, acomp, az, az_send, az_recv)

    for d in range(depth_count):

        def gone(k, carry):
            pair(d, lax.rem(mine + k, m)).wait_send()
            return carry

        lax.fori_loop(1, m, gone, 0)


def body(states, adjoints, kernels, biases, coarse_gain):
    rows, flat = states.shape[2], states.shape[3]
    depth_count, ch = kernels.shape[0], kernels.shape[-1]
    cells = rows * flat // ch
    n, m = lax.axis_size("layer"), lax.axis_size("dp")
    images = m * states.shape[1]
    c = rows
    top = flat // (2 * ch) // group * rows
    planes = n // group
    vmem = pl.BlockSpec(memory_space=pltpu.VMEM)
    anywhere = pl.BlockSpec(memory_space=pl.ANY)
    hbm = pl.BlockSpec(memory_space=pltpu.HBM)
    wide = 2 * ch
    dma = pltpu.SemaphoreType.DMA
    results = pl.pallas_call(
        functools.partial(kernel, n, m, c, images),
        out_shape=(
            jax.ShapeDtypeStruct((rows, flat), F32),
            jax.ShapeDtypeStruct((rows, flat), F32),
            jax.ShapeDtypeStruct(kernels.shape, F32),
            jax.ShapeDtypeStruct(biases.shape, F32),
        ),
        in_specs=[hbm] * 5,
        out_specs=(vmem,) * 4,
        scratch_shapes=[
            pltpu.VMEM((rows, flat), F32),
            pltpu.VMEM((rows, flat), F32),
            pltpu.VMEM(kernels.shape, BF16),
            pltpu.VMEM(biases.shape, F32),
            pltpu.VMEM(coarse_gain.shape, F32),
            dma((5,)),
            pltpu.VMEM((depth_count, cells, 3 * ch), BF16),
            pltpu.VMEM((depth_count, cells, ch), F32),
            pltpu.VMEM((depth_count, cells, 3 * ch), BF16),
            pltpu.VMEM((depth_count, 3 * ch, 3 * ch), BF16),
            pltpu.VMEM((group, top + 8, wide), F32),
            pltpu.VMEM((group, top, wide), F32),
            pltpu.VMEM((group, top + 8, wide), F32),
            pltpu.VMEM((group, top, wide), F32),
            pltpu.VMEM((top + 8, wide), F32),
            pltpu.VMEM((top + 8, wide), F32),
            pltpu.VMEM((planes, top + 8, wide), F32),
            pltpu.VMEM((planes, top + 8, wide), F32),
            pltpu.VMEM((group, top, wide), F32),
            pltpu.VMEM((group, top, wide), F32),
            pltpu.VMEM((group, top, wide), F32),
            pltpu.VMEM((group, top, wide), F32),
            pltpu.VMEM((m, depth_count, 3 * ch + 8, 3 * ch), F32),
        ]
        + [dma((group,))] * 8
        + [dma((planes,))] * 4
        + [dma((m, depth_count))] * 2,
        compiler_params=pltpu.CompilerParams(
            collective_id=0, has_side_effects=True, vmem_limit_bytes=48 * 1024 * 1024
        ),
    )(states, adjoints, kernels, biases, coarse_gain)
    return pl.pallas_call(
        store,
        out_shape=(
            jax.ShapeDtypeStruct(states.shape, F32),
            jax.ShapeDtypeStruct(states.shape, F32),
            jax.ShapeDtypeStruct(kernels.shape, F32),
            jax.ShapeDtypeStruct(biases.shape, F32),
        ),
        in_specs=[anywhere] * 4,
        out_specs=(hbm,) * 4,
        scratch_shapes=[dma((4,))],
        compiler_params=pltpu.CompilerParams(vmem_limit_bytes=1024 * 1024),
    )(*results)


def solution(mesh):
    return jax.shard_map(
        body,
        mesh=mesh,
        in_specs=(
            P("layer", "dp", None, None),
            P("layer", "dp", None, None),
            P("layer", None, None, None, None),
            P("layer", None),
            P("layer", None),
        ),
        out_specs=(
            P("layer", "dp", None, None),
            P("layer", "dp", None, None),
            P("layer", None, None, None, None),
            P("layer", None),
        ),
        check_vma=False,
    )
```

time: 32.8 us -> 26 us (0.79)
  the two profiles are of different devices: /device:TPU:24 before, /device:TPU:0 now
where the time goes in v2:
time: 26 us; the launch traced here: 25.8 us
  Pallas kernels  20.9 us (80%)
  local copies, waits for them, and re-layouts  4.21 us (16%)
  between operations  0.65 us (2%)
    pallas_call x1, Pallas kernels, body(): pl.pallas_call(functools.partial(kernel, n, m, c, images), out_shape=(jax...  19.8 us
    unnamed x10, local copies, waits for them, and re-layouts  4.21 us
    pallas_call x1, Pallas kernels, body(): pl.pallas_call(store, out_shape=(jax.ShapeDtypeStruct(states.shape, F32),...  1.14 us

profile of v2, /device:TPU:0, one launch (start us, length us, event | category | flops | bytes accessed | tf_op | source)
XLA Modules:
  0.0 25.8 jit_solution(8009699976748111798)
XLA Ops:
  0.6 0.0 copy-start
  0.6 1.1 %copy-done = bf16[4,3,3,64,64]{4,3,2,1,0:T(8,128)(2,1)S(1)} copy-done((bf16[4,3,3,64,64]{4,3,2,1,0:T(8,128)(2,1)S(1)}, bf16[4,3,3,64,64]{4,3,2,1,0:T(8,128)(2,1)}, u32[]{:S(2)}) %copy-start) | copy-done | bytes 294936
  1.7 0.0 copy-start.1
  1.7 0.9 %copy-done.1 = f32[1,1,24,1536]{3,2,1,0:T(8,128)S(1)} copy-done((f32[1,1,24,1536]{3,2,1,0:T(8,128)S(1)}, f32[1,1,24,1536]{3,2,1,0:T(8,128)}, u32[]{:S(2)}) %copy-start.1) | copy-done | bytes 147480
  2.6 0.0 copy-start.2
  2.6 0.9 %copy-done.2 = f32[1,1,24,1536]{3,2,1,0:T(8,128)S(1)} copy-done((f32[1,1,24,1536]{3,2,1,0:T(8,128)S(1)}, f32[1,1,24,1536]{3,2,1,0:T(8,128)}, u32[]{:S(2)}) %copy-start.2) | copy-done | bytes 147480
  3.5 0.0 copy-start.3
  3.5 0.7 %copy-done.3 = f32[4,64]{1,0:T(4,128)S(1)} copy-done((f32[4,64]{1,0:T(4,128)S(1)}, f32[4,64]{1,0:T(4,128)}, u32[]{:S(2)}) %copy-start.3) | copy-done | bytes 1048
  4.2 0.0 copy-start.4
  4.2 0.7 %copy-done.4 = f32[1,64]{1,0:T(1,128)S(1)} copy-done((f32[1,64]{1,0:T(1,128)S(1)}, f32[1,64]{1,0:T(1,128)}, u32[]{:S(2)}) %copy-start.4) | copy-done | bytes 280
  4.9 19.8 %shard_map.84 = (f32[24,1536]{1,0:T(8,128)S(1)}, f32[24,1536]{1,0:T(8,128)S(1)}, f32[4,3,3,64,64]{4,3,2,1,0:T(8,128)S(1)}, f32[4,64]{1,0:T(4,128)S(1)}) custom-call(f32[1,1,24,1536]{3,2,1,0:T(8,128)S(1)} %copy-done.1, f32[1,1,24,1536]{3,2,1,0:T(8,128)S(1)} %copy-done.2, bf16[4,3,3,64,64]{4,3,2,1,0:T(8,128)(2,1)S(1)} %copy-done, f32[4,64]{1,0:T(4,128)S(1)} %copy-done.3, ...), custom_call_target="tpu_custom_call" | custom-call | tf_op jit(solution)/shard_map/pallas_call | solution.py:359
  24.6 1.1 %shard_map.85 = (f32[1,1,24,1536]{3,2,1,0:T(8,128)}, f32[1,1,24,1536]{3,2,1,0:T(8,128)}, f32[4,3,3,64,64]{4,3,2,1,0:T(8,128)}, f32[4,64]{1,0:T(4,128)}) custom-call(f32[24,1536]{1,0:T(8,128)S(1)} %get-tuple-element.8.out_s, f32[24,1536]{1,0:T(8,128)S(1)} %get-tuple-element.9.out_a, f32[4,3,3,64,64]{4,3,2,1,0:T(8,128)S(1)} %get-tuple-element.10.out_k, ...), custom_call_target="tpu_custom_call" | custom-call | tf_op jit(solution)/shard_map/pallas_call | solution.py:401
Async XLA Ops:
  0.6 1.1 %copy-start = (bf16[4,3,3,64,64]{4,3,2,1,0:T(8,128)(2,1)S(1)}, bf16[4,3,3,64,64]{4,3,2,1,0:T(8,128)(2,1)}, u32[]{:S(2)}) copy-start(bf16[4,3,3,64,64]{4,3,2,1,0:T(8,128)(2,1)} %ker_any.1) | copy-start | bytes 884740
  1.7 0.9 %copy-start.1 = (f32[1,1,24,1536]{3,2,1,0:T(8,128)S(1)}, f32[1,1,24,1536]{3,2,1,0:T(8,128)}, u32[]{:S(2)}) copy-start(f32[1,1,24,1536]{3,2,1,0:T(8,128)} %st_any.1) | copy-start | bytes 442372
  2.6 0.9 %copy-start.2 = (f32[1,1,24,1536]{3,2,1,0:T(8,128)S(1)}, f32[1,1,24,1536]{3,2,1,0:T(8,128)}, u32[]{:S(2)}) copy-start(f32[1,1,24,1536]{3,2,1,0:T(8,128)} %adj_any.1) | copy-start | bytes 442372
  3.5 0.7 %copy-start.3 = (f32[4,64]{1,0:T(4,128)S(1)}, f32[4,64]{1,0:T(4,128)}, u32[]{:S(2)}) copy-start(f32[4,64]{1,0:T(4,128)} %bias_any.1) | copy-start | bytes 3076
  4.2 0.7 %copy-start.4 = (f32[1,64]{1,0:T(1,128)S(1)}, f32[1,64]{1,0:T(1,128)}, u32[]{:S(2)}) copy-start(f32[1,64]{1,0:T(1,128)} %gain_any.1) | copy-start | bytes 772

commit v3 on v2

--- a/solution.py
+++ b/solution.py
@@ -62,9 +62,9 @@
 
 def kernel(
     n, m, c, images,
-    st_any, adj_any, ker_any, bias_any, gain_any,
+    ends_any, ker_any, bias_any,
     out_s, out_a, out_k, out_b,
-    st, adj, ker, bias, gain, in_sem,
+    st, adj, ker, bias, in_sem,
     xs, acts, s3s, kf, fsend, asend, fin, ain, fcomp, acomp, fz, az, fout, aout, fres, ares, gbuf,
     fs_send, fs_recv, as_send, as_recv, fr_send, fr_recv, ar_send, ar_recv,
     fz_send, fz_recv, az_send, az_recv, g_send, g_recv,
@@ -82,10 +82,9 @@
         for k, (src, dst) in enumerate(
             [
                 (ker_any, ker),
-                (st_any.at[0, 0], st),
+                (ends_any.at[:c], st),
                 (bias_any, bias),
-                (adj_any.at[0, 0], adj),
-                (gain_any, gain),
+                (ends_any.at[c:], adj),
             ]
         )
     ]
@@ -144,8 +143,7 @@
         field = field + step_size * act
 
     loads[3].wait()
-    loads[4].wait()
-    gain_row = gain[...]
+    gain_row = bias[depth_count : depth_count + 1, :]
     zero_row = jnp.zeros_like(gain_row)
     lead = jnp.where(me == 0, zero_row, gain_row)
     tail = jnp.where(me == n - 1, zero_row, gain_row)
@@ -364,15 +362,14 @@
             jax.ShapeDtypeStruct(kernels.shape, F32),
             jax.ShapeDtypeStruct(biases.shape, F32),
         ),
-        in_specs=[hbm] * 5,
+        in_specs=[hbm] * 3,
         out_specs=(vmem,) * 4,
         scratch_shapes=[
             pltpu.VMEM((rows, flat), F32),
             pltpu.VMEM((rows, flat), F32),
             pltpu.VMEM(kernels.shape, BF16),
-            pltpu.VMEM(biases.shape, F32),
-            pltpu.VMEM(coarse_gain.shape, F32),
-            dma((5,)),
+            pltpu.VMEM((depth_count + 1, ch), F32),
+            dma((4,)),
             pltpu.VMEM((depth_count, cells, 3 * ch), BF16),
             pltpu.VMEM((depth_count, cells, ch), F32),
             pltpu.VMEM((depth_count, cells, 3 * ch), BF16),
@@ -397,7 +394,11 @@
         compiler_params=pltpu.CompilerParams(
             collective_id=0, has_side_effects=True, vmem_limit_bytes=48 * 1024 * 1024
         ),
-    )(states, adjoints, kernels, biases, coarse_gain)
+    )(
+        jnp.concatenate([states[0, 0], adjoints[0, 0]]),
+        kernels,
+        jnp.concatenate([biases, coarse_gain]),
+    )
     return pl.pallas_call(
         store,
         out_shape=(

time: 26 us -> 24.5 us (0.942)
  local copies, waits for them, and re-layouts: 4.21 us -> 1.06 us
  other arithmetic: 0 us -> 1.71 us
    unnamed x10 -> x2, local copies, waits for them, and re-layouts: 4.21 us -> 1.06 us
    concatenate x0 -> x2, other arithmetic: none -> 1.71 us  [the longest x1 1 us: body(): jnp.concatenate([states[0, 0], adjoints[0, 0]])]
where the time goes in v3:
time: 24.5 us; the launch traced here: 24.3 us
  Pallas kernels  20.9 us (85%)
  other arithmetic  1.71 us (7%)
  local copies, waits for them, and re-layouts  1.06 us (4%)
  between operations  0.65 us (3%)
    pallas_call x1, Pallas kernels, body(): pl.pallas_call(functools.partial(kernel, n, m, c, images), out_shape=(jax...  19.7 us
    pallas_call x1, Pallas kernels, body(): pl.pallas_call(store, out_shape=(jax.ShapeDtypeStruct(states.shape, F32),...  1.14 us
    unnamed x2, local copies, waits for them, and re-layouts  1.06 us
    concatenate x1, other arithmetic, body(): jnp.concatenate([states[0, 0], adjoints[0, 0]])  1 us
    concatenate x1, other arithmetic, body(): jnp.concatenate([biases, coarse_gain])  0.71 us

profile of v3, /device:TPU:0, one launch (start us, length us, event | category | flops | bytes accessed | tf_op | source)
XLA Modules:
  0.0 24.3 jit_solution(8864159260581923751)
XLA Ops:
  0.6 0.7 %pad_maximum_fusion.1.bias_any = f32[5,64]{1,0:T(8,128)S(1)} fusion(f32[1,64]{1,0:T(1,128)} %param.9, f32[4,64]{1,0:T(4,128)} %param.8), kind=kLoop, calls=%fused_computation.1 | loop fusion | flops 320 | bytes 2560 | tf_op jit(solution)/shard_map/concatenate | solution.py:400
  1.3 1.0 %pad_maximum_fusion.ends_any = f32[48,1536]{1,0:T(8,128)S(1)} fusion(f32[24,1536]{1,0:T(8,128)} %bitcast.2, f32[24,1536]{1,0:T(8,128)} %bitcast.3), kind=kLoop, calls=%fused_computation | loop fusion | flops 73728 | bytes 589824 | tf_op jit(solution)/shard_map/concatenate | solution.py:398
  2.3 0.0 copy-start
  2.4 1.1 %copy-done = bf16[4,3,3,64,64]{4,3,2,1,0:T(8,128)(2,1)S(1)} copy-done((bf16[4,3,3,64,64]{4,3,2,1,0:T(8,128)(2,1)S(1)}, bf16[4,3,3,64,64]{4,3,2,1,0:T(8,128)(2,1)}, u32[]{:S(2)}) %copy-start) | copy-done | bytes 294936
  3.4 19.7 %shard_map.84 = (f32[24,1536]{1,0:T(8,128)S(1)}, f32[24,1536]{1,0:T(8,128)S(1)}, f32[4,3,3,64,64]{4,3,2,1,0:T(8,128)S(1)}, f32[4,64]{1,0:T(4,128)S(1)}) custom-call(f32[48,1536]{1,0:T(8,128)S(1)} %pad_maximum_fusion.ends_any, bf16[4,3,3,64,64]{4,3,2,1,0:T(8,128)(2,1)S(1)} %copy-done, f32[5,64]{1,0:T(8,128)S(1)} %pad_maximum_fusion.1.bias_any), custom_call_target="tpu_custom_call" | custom-call | tf_op jit(solution)/shard_map/pallas_call | solution.py:357
  23.2 1.1 %shard_map.85 = (f32[1,1,24,1536]{3,2,1,0:T(8,128)}, f32[1,1,24,1536]{3,2,1,0:T(8,128)}, f32[4,3,3,64,64]{4,3,2,1,0:T(8,128)}, f32[4,64]{1,0:T(4,128)}) custom-call(f32[24,1536]{1,0:T(8,128)S(1)} %get-tuple-element.8.out_s, f32[24,1536]{1,0:T(8,128)S(1)} %get-tuple-element.9.out_a, f32[4,3,3,64,64]{4,3,2,1,0:T(8,128)S(1)} %get-tuple-element.10.out_k, ...), custom_call_target="tpu_custom_call" | custom-call | tf_op jit(solution)/shard_map/pallas_call | solution.py:402
Async XLA Ops:
  2.3 1.1 %copy-start = (bf16[4,3,3,64,64]{4,3,2,1,0:T(8,128)(2,1)S(1)}, bf16[4,3,3,64,64]{4,3,2,1,0:T(8,128)(2,1)}, u32[]{:S(2)}) copy-start(bf16[4,3,3,64,64]{4,3,2,1,0:T(8,128)(2,1)} %ker_any.1) | copy-start | bytes 884740

commit v4 on v3

--- a/solution.py
+++ b/solution.py
@@ -62,9 +62,8 @@
 
 def kernel(
     n, m, c, images,
-    ends_any, ker_any, bias_any,
+    ends, ker, bias,
     out_s, out_a, out_k, out_b,
-    st, adj, ker, bias, in_sem,
     xs, acts, s3s, kf, fsend, asend, fin, ain, fcomp, acomp, fz, az, fout, aout, fres, ares, gbuf,
     fs_send, fs_recv, as_send, as_recv, fr_send, fr_recv, ar_send, ar_recv,
     fz_send, fz_recv, az_send, az_recv, g_send, g_recv,
@@ -73,23 +72,10 @@
     mine = lax.axis_index("dp")
     depth_count = ker.shape[0]
     ch = ker.shape[-1]
-    flat = st.shape[1]
+    flat = ends.shape[1]
+    st, adj = ends.at[:c], ends.at[c:]
     cells = c * flat // ch
     top = asend.shape[1]
-
-    loads = [
-        pltpu.make_async_copy(src, dst, in_sem.at[k])
-        for k, (src, dst) in enumerate(
-            [
-                (ker_any, ker),
-                (ends_any.at[:c], st),
-                (bias_any, bias),
-                (ends_any.at[c:], adj),
-            ]
-        )
-    ]
-    for load in loads:
-        load.start()
 
     barrier = pltpu.get_barrier_semaphore()
 
@@ -116,7 +102,6 @@
     row = lax.rem(lax.broadcasted_iota(jnp.int32, (cells, ch), 0), c)
     has_left = row > 0
     has_right = row < c - 1
-    loads[0].wait()
 
     for d in range(depth_count):
         kf[d] = jnp.concatenate(
@@ -127,10 +112,8 @@
             axis=1,
         )
 
-    loads[1].wait()
     start = cells_of(st[...], c, ch)
     field = start
-    loads[2].wait()
     for d in range(depth_count):
         left = jnp.where(has_left, down(field, 1), 0.0)
         right = jnp.where(has_right, up(field, 1), 0.0)
@@ -142,7 +125,6 @@
         acts[d] = act
         field = field + step_size * act
 
-    loads[3].wait()
     gain_row = bias[depth_count : depth_count + 1, :]
     zero_row = jnp.zeros_like(gain_row)
     lead = jnp.where(me == 0, zero_row, gain_row)
@@ -362,14 +344,9 @@
             jax.ShapeDtypeStruct(kernels.shape, F32),
             jax.ShapeDtypeStruct(biases.shape, F32),
         ),
-        in_specs=[hbm] * 3,
+        in_specs=[vmem] * 3,
         out_specs=(vmem,) * 4,
         scratch_shapes=[
-            pltpu.VMEM((rows, flat), F32),
-            pltpu.VMEM((rows, flat), F32),
-            pltpu.VMEM(kernels.shape, BF16),
-            pltpu.VMEM((depth_count + 1, ch), F32),
-            dma((4,)),
             pltpu.VMEM((depth_count, cells, 3 * ch), BF16),
             pltpu.VMEM((depth_count, cells, ch), F32),
             pltpu.VMEM((depth_count, cells, 3 * ch), BF16),

time: 24.5 us -> 24 us (0.980)
  Pallas kernels: 20.9 us -> 20.3 us
    pallas_call x1, Pallas kernels: 19.7 us -> 19.2 us  [body(): pl.pallas_call(functools.partial(kernel, n, m, c, images), out_shape=(jax...]
where the time goes in v4:
time: 24 us; the launch traced here: 23.8 us
  Pallas kernels  20.3 us (85%)
  other arithmetic  1.71 us (7%)
  local copies, waits for them, and re-layouts  1.06 us (4%)
  between operations  0.65 us (3%)
    pallas_call x1, Pallas kernels, body(): pl.pallas_call(functools.partial(kernel, n, m, c, images), out_shape=(jax...  19.2 us
    pallas_call x1, Pallas kernels, body(): pl.pallas_call(store, out_shape=(jax.ShapeDtypeStruct(states.shape, F32),...  1.14 us
    unnamed x2, local copies, waits for them, and re-layouts  1.06 us
    concatenate x1, other arithmetic, body(): jnp.concatenate([states[0, 0], adjoints[0, 0]])  1 us
    concatenate x1, other arithmetic, body(): jnp.concatenate([biases, coarse_gain])  0.71 us

profile of v4, /device:TPU:0, one launch (start us, length us, event | category | flops | bytes accessed | tf_op | source)
XLA Modules:
  0.0 23.8 jit_solution(4520617746767614349)
XLA Ops:
  0.6 0.7 %pad_maximum_fusion.1.bias = f32[5,64]{1,0:T(8,128)S(1)} fusion(f32[1,64]{1,0:T(1,128)} %param.9, f32[4,64]{1,0:T(4,128)} %param.8), kind=kLoop, calls=%fused_computation.1 | loop fusion | flops 320 | bytes 2560 | tf_op jit(solution)/shard_map/concatenate | solution.py:377
  1.3 1.0 %pad_maximum_fusion.ends = f32[48,1536]{1,0:T(8,128)S(1)} fusion(f32[24,1536]{1,0:T(8,128)} %bitcast.2, f32[24,1536]{1,0:T(8,128)} %bitcast.3), kind=kLoop, calls=%fused_computation | loop fusion | flops 73728 | bytes 589824 | tf_op jit(solution)/shard_map/concatenate | solution.py:375
  2.3 0.0 copy-start
  2.4 1.1 %copy-done = bf16[4,3,3,64,64]{4,3,2,1,0:T(8,128)(2,1)S(1)} copy-done((bf16[4,3,3,64,64]{4,3,2,1,0:T(8,128)(2,1)S(1)}, bf16[4,3,3,64,64]{4,3,2,1,0:T(8,128)(2,1)}, u32[]{:S(2)}) %copy-start) | copy-done | bytes 294936
  3.4 19.2 %shard_map.84 = (f32[24,1536]{1,0:T(8,128)S(1)}, f32[24,1536]{1,0:T(8,128)S(1)}, f32[4,3,3,64,64]{4,3,2,1,0:T(8,128)S(1)}, f32[4,64]{1,0:T(4,128)S(1)}) custom-call(f32[48,1536]{1,0:T(8,128)S(1)} %pad_maximum_fusion.ends, bf16[4,3,3,64,64]{4,3,2,1,0:T(8,128)(2,1)S(1)} %copy-done, f32[5,64]{1,0:T(8,128)S(1)} %pad_maximum_fusion.1.bias), custom_call_target="tpu_custom_call" | custom-call | tf_op jit(solution)/shard_map/pallas_call | solution.py:339
  22.6 1.1 %shard_map.85 = (f32[1,1,24,1536]{3,2,1,0:T(8,128)}, f32[1,1,24,1536]{3,2,1,0:T(8,128)}, f32[4,3,3,64,64]{4,3,2,1,0:T(8,128)}, f32[4,64]{1,0:T(4,128)}) custom-call(f32[24,1536]{1,0:T(8,128)S(1)} %get-tuple-element.8.out_s, f32[24,1536]{1,0:T(8,128)S(1)} %get-tuple-element.9.out_a, f32[4,3,3,64,64]{4,3,2,1,0:T(8,128)S(1)} %get-tuple-element.10.out_k, ...), custom_call_target="tpu_custom_call" | custom-call | tf_op jit(solution)/shard_map/pallas_call | solution.py:379
Async XLA Ops:
  2.3 1.1 %copy-start = (bf16[4,3,3,64,64]{4,3,2,1,0:T(8,128)(2,1)S(1)}, bf16[4,3,3,64,64]{4,3,2,1,0:T(8,128)(2,1)}, u32[]{:S(2)}) copy-start(bf16[4,3,3,64,64]{4,3,2,1,0:T(8,128)(2,1)} %ker.1) | copy-start | bytes 884740
